TPU v7x, 256 devices: a whole 4x4x8 slice. The times are simulated.
256 devices in a mesh: section: 16 (over x, y), expert: 16 (over z, core).
Axes of the slice: x: 4, y: 4, z: 8, core: 2. Of those that a mesh axis runs over, the one named last changes fastest.
Arguments:
- tokens: bfloat16 [16, 256, 7168], P('section', 'expert'), may hold values from -6 to 6
- norm_gain: float32 [16, 7168], P('section'), may hold values from 0.1 to 1.9
- gate_weight: bfloat16 [16, 7168, 4096], P('section', None, 'expert'), may hold values from -0.0625 to 0.0625
- up_weight: bfloat16 [16, 7168, 4096], P('section', None, 'expert'), may hold values from -0.0625 to 0.0625
- down_weight: bfloat16 [16, 4096, 7168], P('section', 'expert'), may hold values from -0.1875 to 0.1875
- block_scales: int32 [16, 3, 56, 32], P('section', None, None, 'expert'), may hold values from -1 to 1
- routes: int32 [16, 2, 256, 2], P('section', None, 'expert'), may hold values from 0 to 3, all different within a row; in each aligned block of 16 rows (0 to 15, 16 to 31, ..., all dimensions but the last counted through in order) at most 12 rows name the same one
- route_weights: bfloat16 [16, 2, 256, 2], P('section', None, 'expert'), may hold values from 0.19921875 to 1
Outputs:
- final: bfloat16 [16, 256, 7168], P('section', 'expert')
Inputs may be any that keep to these rules, and one draw needn't show every extreme that they name: `routes`: each token names 2 different experts. For each section and step, the 16 tokens of one device name no expert more than 12 times.
All inputs are finite; a program needn't handle non-finite values.
Results may differ from a plain program's by a relative error of at most 0.025.
Values may be sent and summed in bfloat16 or wider, within the bound.
No kernel may reach another device: no remote copies, remote signals or barrier semaphores. Data moves between devices by JAX's collectives and lax.ppermute only.
A program may use at most 128 MiB of HBM per device.

v0:
```python
import jax
import jax.numpy as jnp
from jax import lax
from jax.sharding import PartitionSpec as P

SPLIT = 4
TICKS = 2


def from_behind(shard, axis, by):
    length = lax.axis_size(axis)
    return lax.ppermute(shard, axis, [(i, (i + by) % length) for i in range(length)])


def dequantize(stored, exponents):
    height, span_cols = stored.shape
    factor = jnp.exp2(exponents.astype(jnp.float32))
    blocked = stored.reshape(height // 128, 128, span_cols // 128, 128).astype(jnp.float32)
    return (blocked * factor[:, None, :, None]).reshape(height, span_cols).astype(jnp.bfloat16)


def rms_normed(current, norm_gain):
    values = current.astype(jnp.float32)
    mean_sq = jnp.mean(values * values, axis=-1, keepdims=True)
    return (values * lax.rsqrt(mean_sq + 1e-06) * norm_gain).astype(jnp.bfloat16)


def expert_share(inputs, weight_rows, gate_full, up_full, down_full):
    gate_out = jnp.dot(inputs, gate_full, preferred_element_type=jnp.float32)
    up_out = jnp.dot(inputs, up_full, preferred_element_type=jnp.float32)
    hidden = (jax.nn.silu(gate_out) * up_out).astype(jnp.bfloat16)
    product = jnp.dot(hidden, down_full, preferred_element_type=jnp.float32)
    return (product * weight_rows[:, None]).astype(jnp.bfloat16)


def per_device(
    tokens, norm_gain, gate_weight, up_weight, down_weight, block_scales, routes, route_weights
):
    groups = lax.axis_size("expert")
    experts = groups // SPLIT
    own_expert = lax.axis_index("expert") // SPLIT
    scales = block_scales[0]
    gate_full = dequantize(gate_weight[0], scales[0])
    up_full = dequantize(up_weight[0], scales[1])
    down_full = dequantize(down_weight[0], scales[2].T)
    current = tokens[0]
    expert_ids = jnp.arange(experts, dtype=jnp.int32)
    for tick_index in range(TICKS):
        normed = rms_normed(current, norm_gain[0])
        chosen = routes[0, tick_index]
        matches = (chosen[:, :, None] == expert_ids[None, None, :]).astype(jnp.float32)
        token_weight = jnp.sum(
            matches * route_weights[0, tick_index].astype(jnp.float32)[:, :, None], axis=1
        )
        weight_table = token_weight.astype(jnp.bfloat16)
        all_rows, all_table = (
            lax.all_gather(normed, "expert", axis=0, tiled=True),
            lax.all_gather(weight_table, "expert", axis=0, tiled=True),
        )
        select = (expert_ids == own_expert).astype(jnp.float32)
        own_weight = jnp.sum(all_table.astype(jnp.float32) * select[None, :], axis=1)
        terms = expert_share(all_rows, own_weight, gate_full, up_full, down_full).astype(
            jnp.float32
        )
        update = lax.psum_scatter(
            terms.astype(jnp.bfloat16), "expert", scatter_dimension=0, tiled=True
        ).astype(jnp.float32)
        current = (current.astype(jnp.float32) + update).astype(jnp.bfloat16)
        current = from_behind(current, "section", 1)
    return current[None]


def solution(mesh):
    in_specs = (
        P("section", "expert", None),
        P("section", None),
        P("section", None, "expert"),
        P("section", None, "expert"),
        P("section", "expert", None),
        P("section", None, None, "expert"),
        P("section", None, "expert", None),
        P("section", None, "expert", None),
    )
    out_specs = P("section", "expert", None)
    return jax.shard_map(
        per_device, mesh=mesh, in_specs=in_specs, out_specs=out_specs, check_vma=False
    )
```

profile of v0, /device:TPU:0, one launch (start us, length us, event | category | flops | bytes accessed | tf_op | source)
XLA Modules:
  0.0 291.6 jit_solution(6469456829982880243)
XLA Ops:
  6.5 1.1 fusion.11
  7.7 1.8 fusion.13
  9.5 0.7 bitcast_convert_fusion.1
  10.2 0.7 slice_bitcast_fusion.1
  10.9 18.2 %all-gather = bf16[16,16,4]{1,2,0:T(4,128)(2,1)S(1)} all-gather(bf16[1,16,4]{1,2,0:T(4,128)(2,1)S(1)} %bitcast.91), channel_id=1, replica_groups=mesh['section'=16,'expert'=16] {'expert'}, dimensions={0}, use_global_device_ids=true | all-gather | bytes 2176 | tf_op jit(solution)/shard_map/all_gather | solution.py:58
  29.1 0.1 reshape.99
  29.2 14.4 %all-gather.1 = bf16[16,16,4]{1,2,0:T(4,128)(2,1)S(1)} all-gather(bf16[1,16,4]{1,2,0:T(4,128)(2,1)S(1)} %bitcast.92), channel_id=1, replica_groups=mesh['section'=16,'expert'=16] {'expert'}, dimensions={0}, use_global_device_ids=true | all-gather | bytes 2176 | tf_op jit(solution)/shard_map/all_gather | solution.py:58
  43.7 0.1 reshape.100
  43.8 0.7 exponential_bitcast_fusion
  44.5 0.1 copy.35
  44.6 0.1 copy.36
  44.8 7.3 %all-gather.5.cloned.1.call-done = bf16[256,7168]{1,0:T(8,128)(2,1)} async-done(((bf16[16,7168]{1,0:T(8,128)(2,1)}), bf16[256,7168]{1,0:T(8,128)(2,1)}) %all-gather.5.cloned.1.call-update) | async-done | bytes 3670032 | tf_op jit(solution)/shard_map/all_gather | solution.py:57
  52.1 1.9 mul.136
  54.1 5.9 %fusion.31 = f32[256,256]{1,0:T(8,128)S(1)} fusion(bf16[256,7168]{1,0:T(8,128)(2,1)} %all-gather.5.cloned.1.call-done, f32[896,8,2,128]{3,2,1,0:T(2,128)S(1)} %bitcast.84, bf16[1,7168,256]{2,1,0:T(8,128)(2,1)S(1)} %copy-done.1), kind=kOutput, calls=%fused_computation.63 | convolution fusion | flops 945029120 | bytes 14942208 | tf_op jit(solution)/shard_map/dot_general | solution.py:29
  60.0 4.9 %mul.140 = f32[56,128,2,128]{3,2,1,0:T(2,128)} broadcast(f32[56,2]{1,0:T(8,128)S(1)} %copy.36), dimensions={0,2} | broadcast | bytes 7340480 | tf_op jit(solution)/shard_map/mul | solution.py:19
  64.9 3.6 %mul.144 = f32[2,128,56,128]{3,2,1,0:T(8,128)} broadcast(f32[2,56]{1,0:T(2,128)S(1)} %get-tuple-element.7), dimensions={0,2} | broadcast | bytes 7340480 | tf_op jit(solution)/shard_map/mul | solution.py:19
  68.5 14.2 %fusion = bf16[256,7168]{1,0:T(8,128)(2,1)} fusion(f32[256]{0:T(256)S(1)} %get-tuple-element.6, bf16[256,7168]{1,0:T(8,128)(2,1)} %all-gather.5.cloned.1.call-done, f32[256,256]{1,0:T(8,128)S(1)} %fusion.31, f32[896,8,2,128]{3,2,1,0:T(2,128)} %bitcast.82, bf16[1,7168,256]{2,1,0:T(8,128)(2,1)} %param.11, f32[32,8,56,128]{3,2,1,0:T(8,128)} %bitcast.86, ...), kind=kOutput, calls=%fused_computation.2 | convolution fusion | flops 1894121472 | bytes 29623296 | tf_op jit(solution)/shard_map/dot_general | solution.py:32
  82.8 60.9 %reduce-scatter.3.cloned.1.call-done = bf16[16,7168]{1,0:T(8,128)(2,1)} async-done(((bf16[256,7168]{1,0:T(8,128)(2,1)}), bf16[16,7168]{1,0:T(8,128)(2,1)}) %reduce-scatter.3.cloned.1.call-update) | async-done | bytes 229392 | tf_op jit(solution)/shard_map/reduce_scatter | solution.py:65
  143.8 1.0 fusion.14
  144.8 1.6 collective-permute-start
  146.3 7.8 %collective-permute-done = bf16[16,7168]{1,0:T(8,128)(2,1)S(1)} collective-permute-done((bf16[16,7168]{1,0:T(8,128)(2,1)S(1)}, bf16[16,7168]{1,0:T(8,128)(2,1)S(1)}, u32[]{:S(2)}, u32[]{:S(2)}) %collective-permute-start) | collective-permute-done | bytes 229408 | tf_op jit(solution)/shard_map/ppermute | solution.py:12
  154.2 0.2 fusion.7
  154.4 0.8 fusion.9
  155.2 0.2 reduce-scatter.5.cloned.1.call-start
  155.4 37.4 %all-gather.7.cloned.1.call-done = bf16[256,7168]{1,0:T(8,128)(2,1)} async-done(((bf16[16,7168]{1,0:T(8,128)(2,1)}), bf16[256,7168]{1,0:T(8,128)(2,1)}) %all-gather.7.cloned.1.call-update) | async-done | bytes 3670032 | tf_op jit(solution)/shard_map/all_gather | solution.py:57
  192.9 6.4 %fusion.29 = f32[256,256]{1,0:T(8,128)S(1)} fusion(bf16[256,7168]{1,0:T(8,128)(2,1)} %all-gather.7.cloned.1.call-done, f32[896,8,2,128]{3,2,1,0:T(2,128)} %bitcast.85, bf16[1,7168,256]{2,1,0:T(8,128)(2,1)} %param.10), kind=kOutput, calls=%fused_computation.62 | convolution fusion | flops 945029120 | bytes 14942208 | tf_op jit(solution)/shard_map/dot_general | solution.py:29
  199.3 14.2 %fusion.1 = bf16[256,7168]{1,0:T(8,128)(2,1)} fusion(f32[256]{0:T(256)S(1)} %get-tuple-element.5, bf16[256,7168]{1,0:T(8,128)(2,1)} %all-gather.7.cloned.1.call-done, f32[256,256]{1,0:T(8,128)S(1)} %fusion.29, f32[896,8,2,128]{3,2,1,0:T(2,128)} %bitcast.83, bf16[1,7168,256]{2,1,0:T(8,128)(2,1)} %param.11, f32[32,8,56,128]{3,2,1,0:T(8,128)} %bitcast.87, ...), kind=kOutput, calls=%fused_computation.3 | convolution fusion | flops 1894121472 | bytes 29623296 | tf_op jit(solution)/shard_map/dot_general | solution.py:32
  213.6 60.5 %reduce-scatter.5.cloned.1.call-done = bf16[16,7168]{1,0:T(8,128)(2,1)} async-done(((bf16[256,7168]{1,0:T(8,128)(2,1)}), bf16[16,7168]{1,0:T(8,128)(2,1)}) %reduce-scatter.5.cloned.1.call-update) | async-done | bytes 229392 | tf_op jit(solution)/shard_map/reduce_scatter | solution.py:65
  274.0 1.0 fusion.10
  275.0 1.7 collective-permute-start.1
  276.7 7.7 %collective-permute-done.1 = bf16[16,7168]{1,0:T(8,128)(2,1)S(1)} collective-permute-done((bf16[16,7168]{1,0:T(8,128)(2,1)S(1)}, bf16[16,7168]{1,0:T(8,128)(2,1)S(1)}, u32[]{:S(2)}, u32[]{:S(2)}) %collective-permute-start.1) | collective-permute-done | bytes 229408 | tf_op jit(solution)/shard_map/ppermute | solution.py:12
  284.4 0.7 copy.56
  (23 shorter events, 0.4 us)
Async XLA Ops:
  6.5 45.5 %all-gather.5.cloned.1.call-start = ((), (), s32[]{:S(2)}) async-start(), calls=%async_computation.2 | async-start | bytes 3899392 | tf_op jit(solution)/shard_map/all_gather | solution.py:57
  9.4 134.3 %reduce-scatter.3.cloned.1.call-start = ((), (), s32[]{:S(2)}) async-start(), calls=%async_computation.3 | async-start | bytes 3899392 | tf_op jit(solution)/shard_map/reduce_scatter | solution.py:65
  52.1 2.0 copy-start.1
  54.0 6.0 %copy-start = (f32[56,128,2,128]{3,2,1,0:T(2,128)}, f32[56,128,2,128]{3,2,1,0:T(2,128)S(1)}, u32[]{:S(2)}) copy-start(f32[56,128,2,128]{3,2,1,0:T(2,128)S(1)} %mul.136) | copy-start | bytes 22020100
  82.7 61.0 %copy-start.2 = (bf16[1,16,7168]{2,1,0:T(8,128)(2,1)S(1)}, bf16[1,16,7168]{2,1,0:T(8,128)(2,1)}, u32[]{:S(2)}) copy-start(bf16[1,16,7168]{2,1,0:T(8,128)(2,1)} %param.8) | copy-start | bytes 688132
  82.8 71.6 %copy-start.3 = (f32[1,7168]{1,0:T(1,128)S(1)}, f32[1,7168]{1,0:T(1,128)}, u32[]{:S(2)}) copy-start(f32[1,7168]{1,0:T(1,128)} %param.9) | copy-start | bytes 86020
  82.8 110.1 %all-gather.7.cloned.1.call-start = ((), (), s32[]{:S(2)}) async-start(), calls=%async_computation.4 | async-start | bytes 3899392 | tf_op jit(solution)/shard_map/all_gather | solution.py:57
  144.8 9.4 %collective-permute-start = (bf16[16,7168]{1,0:T(8,128)(2,1)S(1)}, bf16[16,7168]{1,0:T(8,128)(2,1)S(1)}, u32[]{:S(2)}, u32[]{:S(2)}) collective-permute-start(bf16[16,7168]{1,0:T(8,128)(2,1)S(1)} %fusion.14), channel_id=1, source_target_pairs={{0,16},{16,32},{32,48},{48,64},{64,80},{80,96},{96,112},{112,128},... | collective-permute-start | bytes 688136 | tf_op jit(solution)/shard_map/ppermute | solution.py:12
  155.2 118.8 %reduce-scatter.5.cloned.1.call-start = ((), (), s32[]{:S(2)}) async-start(), calls=%async_computation.5 | async-start | bytes 3899392 | tf_op jit(solution)/shard_map/reduce_scatter | solution.py:65
  275.0 9.4 %collective-permute-start.1 = (bf16[16,7168]{1,0:T(8,128)(2,1)S(1)}, bf16[16,7168]{1,0:T(8,128)(2,1)S(1)}, u32[]{:S(2)}, u32[]{:S(2)}) collective-permute-start(bf16[16,7168]{1,0:T(8,128)(2,1)S(1)} %fusion.10), channel_id=1, source_target_pairs={{0,16},{16,32},{32,48},{48,64},{64,80},{80,96},{96,112},{112,128},... | collective-permute-start | bytes 688136 | tf_op jit(solution)/shard_map/ppermute | solution.py:12
Sparse Core Ops, SparseCore 0:
  9.6 42.4 all-gather.4
  82.9 60.8 reduce-scatter.2
  155.3 37.4 all-gather.6
  213.7 60.2 reduce-scatter.4
where the time goes:
time: 293 us; the launch traced here: 292 us
  waiting for transfers between devices  182 us (62%)
  matrix products  40.8 us (14%)
  blocking collectives  32.7 us (11%)
  between operations  13.2 us (5%)
  local copies, waits for them, and re-layouts  12.3 us (4%)
  other arithmetic  7.38 us (3%)
  starting transfers between devices  3.6 us (1%)
    reduce_scatter x2, waiting for transfers between devices, per_device(): lax.psum_scatter(terms.astype(jnp.bfloat16), 'expert', scatter_dimension=...  121 us
    all_gather x2, waiting for transfers between devices, per_device(): lax.all_gather(normed, 'expert', axis=0, tiled=True)  44.7 us
    all_gather x2, blocking collectives, per_device(): lax.all_gather(weight_table, 'expert', axis=0, tiled=True)  32.7 us
    dot_general x2, matrix products, expert_share(): product = jnp.dot(hidden, down_full, preferred_element_type=jnp.float32)  28.5 us
    ppermute x2, waiting for transfers between devices, from_behind(): lax.ppermute(shard, axis, [(i, (i + by) % length) for i in range(length)])  15.5 us
    dot_general x2, matrix products, expert_share(): gate_out = jnp.dot(inputs, gate_full, preferred_element_type=jnp.float32)  12.3 us
    mul x3, local copies, waits for them, and re-layouts, dequantize(): blocked * factor[:, None, :, None]  10.4 us
  transfers between devices with their start and end apart: 6, of which 6 were waited for; matrix products, arithmetic and copies ran while one was open for 1% of the time, Pallas kernels for 0%

commit v1 on v0

v1 whole, which is shorter than its diff:
```python
import jax
import jax.numpy as jnp
from jax import lax
from jax.experimental import pallas as pl
from jax.experimental.pallas import tpu as pltpu
from jax.sharding import PartitionSpec as P

SPLIT = 4
TICKS = 2
LANES = 128
VMEM_LIMIT = 44 * 1024 * 1024
F32 = jnp.float32
BF16 = jnp.bfloat16


def along_z(shard, by):
    length = lax.axis_size("expert")
    return lax.ppermute(
        shard, "expert", [(i, (i + 2 * by) % length) for i in range(length)]
    )


def other_core(shard):
    length = lax.axis_size("expert")
    return lax.ppermute(shard, "expert", [(i, i ^ 1) for i in range(length)])


def next_section(shard):
    length = lax.axis_size("section")
    return lax.ppermute(shard, "section", [(i, (i + 1) % length) for i in range(length)])


def cut_of(width):
    return width // LANES // 2 * LANES


def gather_first(block):
    far_back, far_ahead = along_z(block, 2), along_z(block, -2)
    return [block, along_z(block, 1), along_z(block, -1), far_back, far_ahead]


def gather_second(first):
    far_back, far_ahead = first[3], first[4]
    cut = cut_of(far_back.shape[1])
    return first + [
        along_z(far_back, 1),
        along_z(far_ahead, -1),
        along_z(far_back[:, :cut], 2),
        along_z(far_ahead[:, cut:], -2),
    ]


def sum_first(outs):
    arrived = [
        along_z(outs[5], -1),
        along_z(outs[6], 1),
        along_z(outs[7], -2),
        along_z(outs[8], 2),
    ]
    near = [along_z(outs[1], -1), along_z(outs[2], 1)]
    return outs, arrived, near


def join_far(outs, arrived):
    rows, width = outs[3].shape
    cut = cut_of(width)

    def kernel(back, ahead, b3, a3, left, right, back_out, ahead_out):
        lo, hi = slice(0, cut), slice(cut, width)
        f = lambda ref, cols: ref[:, cols].astype(F32)
        back_out[:, lo] = (f(back, lo) + f(b3, lo) + left[...].astype(F32)).astype(BF16)
        back_out[:, hi] = (f(back, hi) + f(b3, hi)).astype(BF16)
        ahead_out[:, lo] = (f(ahead, lo) + f(a3, lo)).astype(BF16)
        ahead_out[:, hi] = (f(ahead, hi) + f(a3, hi) + right[...].astype(F32)).astype(BF16)

    shape = jax.ShapeDtypeStruct((rows, width), BF16)
    return pl.pallas_call(
        kernel,
        out_shape=[shape, shape],
        compiler_params=pltpu.CompilerParams(vmem_limit_bytes=VMEM_LIMIT),
        cost_estimate=pl.CostEstimate(
            flops=6 * rows * width, bytes_accessed=14 * rows * width, transcendentals=0
        ),
        name="join_far",
    )(outs[3], outs[4], *arrived)


def sum_second(parts):
    outs, arrived, near = parts
    back, ahead = join_far(outs, arrived)
    return [outs[0], *near, along_z(back, -2), along_z(ahead, 2)]


def total(state, parts):
    value = state.astype(F32)
    for part in parts:
        value = value + part.astype(F32)
    return value.astype(BF16)


def load_rows(pieces, gain, rows_ref, squares_ref):
    height = pieces[0].shape[0]
    width = gain.shape[1]
    cut = cut_of(pieces[0].shape[1])

    def put(ref, at, lo, hi, base):
        held = None
        for c in range(lo, hi, LANES):
            x = ref[:, c - base : c - base + LANES].astype(F32)
            held = x * x if held is None else held + x * x
            rows_ref[at : at + height, c : c + LANES] = (
                x * gain[:, c : c + LANES]
            ).astype(BF16)
        return held

    for n in range(8):
        at = n * height
        if n < 7:
            held = put(pieces[n], at, 0, width, 0)
        else:
            held = put(pieces[7], at, 0, cut, 0) + put(pieces[8], at, cut, width, cut)
        squares_ref[at : at + height, :] = held


def load_table(pieces, width, table_ref):
    height = pieces[0].shape[0]
    cut = cut_of(pieces[0].shape[1])
    for n in range(8):
        ref, lo = (pieces[n], width) if n < 7 else (pieces[8], width - cut)
        table_ref[n * height : (n + 1) * height, :] = ref[:, lo : lo + LANES].astype(F32)


def scaled(block, factor):
    return block * jnp.full(block.shape, factor, F32).astype(BF16)


def experts_share(pieces, gain, weights, factors, table, own_lane):
    width = gain.shape[1]
    hidden_width = weights[0][0].shape[1]
    height = pieces[0].shape[0]
    rows = 8 * height
    blocks, halves = width // LANES, hidden_width // LANES
    per_tile = 8 if blocks % 8 == 0 else 4
    tile = per_tile * LANES
    cut = cut_of(width)
    n_pieces = len(pieces)
    new_table = table is None

    def kernel(*refs):
        lane_ref, factor_refs, ins = refs[0], refs[1:3], refs[3 : 3 + n_pieces]
        gain_ref, rest = refs[3 + n_pieces], refs[4 + n_pieces :]
        gates, ups, downs, rest = rest[0:2], rest[2:4], rest[4:6], rest[6:]
        if not new_table:
            table_in, rest = rest[0], rest[1:]
        outs, table_ref = rest[:9], rest[9]
        rows_ref, tile_ref, down_ref, acc_ref, squares_ref, hidden_ref, weight_ref = rest[10:]

        load_rows(ins, gain_ref, rows_ref, squares_ref)
        if new_table:
            load_table(ins, width, table_ref)
        else:
            table_ref[...] = table_in[...]

        def add_tile(step, first):
            start = pl.multiple_of(step * tile, LANES)
            for which, pair in enumerate((gates, ups)):
                for core in range(2):
                    for a in range(per_tile):
                        for b in range(halves):
                            at = (which * blocks + step * per_tile + a) * halves + b
                            block = pair[core][
                                pl.ds(pl.multiple_of(start + a * LANES, LANES), LANES),
                                b * LANES : (b + 1) * LANES,
                            ]
                            column = (which * 2 + core) * hidden_width + b * LANES
                            tile_ref[
                                a * LANES : (a + 1) * LANES, column : column + LANES
                            ] = scaled(block, factor_refs[core][at])
            product = jnp.dot(
                rows_ref[:, pl.ds(start, tile)], tile_ref[...], preferred_element_type=F32
            )
            acc_ref[...] = product if first else acc_ref[...] + product

        add_tile(0, True)
        lax.fori_loop(1, width // tile, lambda i, c: (add_tile(i, False), c)[1], 0)

        mean = jnp.sum(squares_ref[...], axis=-1, keepdims=True) / width
        factor = lax.rsqrt(mean + 1e-06)
        gate = acc_ref[:, : 2 * hidden_width] * factor
        up = acc_ref[:, 2 * hidden_width :] * factor
        hidden_ref[...] = (gate / (1.0 + jnp.exp(-gate)) * up).astype(BF16)
        lane = lax.broadcasted_iota(jnp.int32, (rows, LANES), 1)
        picked = jnp.where(lane == lane_ref[0], table_ref[...], 0.0)
        weight_ref[...] = jnp.broadcast_to(
            jnp.sum(picked, axis=-1, keepdims=True), (rows, LANES)
        )

        for step in range(width // tile):
            for core in range(2):
                for a in range(per_tile):
                    for b in range(halves):
                        at = (2 * blocks + step * per_tile + a) * halves + b
                        lo = step * tile + a * LANES
                        block = downs[core][b * LANES : (b + 1) * LANES, lo : lo + LANES]
                        row = core * hidden_width + b * LANES
                        down_ref[row : row + LANES, a * LANES : (a + 1) * LANES] = scaled(
                            block, factor_refs[core][at]
                        )
            product = jnp.dot(hidden_ref[...], down_ref[...], preferred_element_type=F32)
            product = (product * weight_ref[:, :1]).astype(BF16)
            lo, hi = step * tile, (step + 1) * tile
            for n in range(7):
                outs[n][:, lo:hi] = product[n * height : (n + 1) * height, :]
            last = product[7 * height :, :]
            if lo < cut:
                outs[7][:, lo : min(hi, cut)] = last[:, : min(hi, cut) - lo]
            if hi > cut:
                outs[8][:, max(lo, cut) - cut : hi - cut] = last[:, max(lo, cut) - lo :]

    smem, vmem = pl.BlockSpec(memory_space=pltpu.SMEM), pl.BlockSpec(memory_space=pltpu.VMEM)
    tables = [] if new_table else [table]
    operands = [*pieces, gain, *weights[0], *weights[1], *weights[2], *tables]
    out_sizes = [(height, width)] * 7 + [(height, cut), (height, width - cut)]
    results = pl.pallas_call(
        kernel,
        in_specs=[smem] * 3 + [vmem] * len(operands),
        out_specs=[vmem] * 10,
        out_shape=[jax.ShapeDtypeStruct(s, BF16) for s in out_sizes]
        + [jax.ShapeDtypeStruct((rows, LANES), F32)],
        scratch_shapes=[
            pltpu.VMEM((rows, width), BF16),
            pltpu.VMEM((tile, 4 * hidden_width), BF16),
            pltpu.VMEM((2 * hidden_width, tile), BF16),
            pltpu.VMEM((rows, 4 * hidden_width), F32),
            pltpu.VMEM((rows, LANES), F32),
            pltpu.VMEM((rows, 2 * hidden_width), BF16),
            pltpu.VMEM((rows, LANES), F32),
        ],
        compiler_params=pltpu.CompilerParams(vmem_limit_bytes=VMEM_LIMIT),
        cost_estimate=pl.CostEstimate(
            flops=12 * rows * width * hidden_width,
            bytes_accessed=12 * width * hidden_width,
            transcendentals=2 * rows * hidden_width,
        ),
        name="experts_share",
    )(own_lane, *factors, *operands)
    return results[:9], results[9]


def weights_table(routes, route_weights, experts):
    ids = jnp.arange(experts, dtype=jnp.int32)
    matches = (routes[..., None] == ids).astype(F32)
    table = jnp.sum(matches * route_weights.astype(F32)[..., None], axis=2)
    table = table.transpose(1, 0, 2).reshape(table.shape[1], TICKS * experts)
    return jnp.pad(table, ((0, 0), (0, LANES - TICKS * experts))).astype(BF16)


def per_device(
    tokens, norm_gain, gate_weight, up_weight, down_weight, block_scales, routes, route_weights
):
    experts = lax.axis_size("expert") // SPLIT
    own_expert = lax.axis_index("expert") // SPLIT
    factors = jnp.exp2(block_scales[0].astype(F32)).reshape(-1)
    factors = (factors, other_core(factors))
    weights = [(w[0], other_core(w[0])) for w in (gate_weight, up_weight, down_weight)]

    state = tokens[0]
    table = weights_table(routes[0], route_weights[0], experts)
    held_table = None
    for tick in range(TICKS):
        rows = state if tick else jnp.concatenate([state, table], axis=1)
        pieces = gather_second(gather_first(rows))
        own_lane = (own_expert + tick * experts).astype(jnp.int32).reshape(1)
        outs, held_table = experts_share(
            pieces, norm_gain, weights, factors, held_table, own_lane
        )
        state = next_section(total(state, sum_second(sum_first(outs))))
    return state[None]


def solution(mesh):
    in_specs = (
        P("section", "expert", None),
        P("section", None),
        P("section", None, "expert"),
        P("section", None, "expert"),
        P("section", "expert", None),
        P("section", None, None, "expert"),
        P("section", None, "expert", None),
        P("section", None, "expert", None),
    )
    out_specs = P("section", "expert", None)
    return jax.shard_map(
        per_device, mesh=mesh, in_specs=in_specs, out_specs=out_specs, check_vma=False
    )
```

time: 293 us -> 185 us (0.63)
  waiting for transfers between devices: 182 us -> 81.5 us
  starting transfers between devices: 3.6 us -> 64.8 us
  matrix products: 40.8 us -> 0 us
  blocking collectives: 32.7 us -> 0 us
  Pallas kernels: 0 us -> 28.8 us
  between operations: 13.2 us -> 0.16 us
  local copies, waits for them, and re-layouts: 12.3 us -> 5.88 us
  other arithmetic: 7.38 us -> 3.39 us
    reduce_scatter x2 -> x0, waiting for transfers between devices: 121 us -> none  [per_device(): lax.psum_scatter(terms.astype(jnp.bfloat16), 'expert', scatter_dimension=...]
    ppermute x2 -> x38, waiting for transfers between devices: 15.5 us -> 81.5 us  [the longest x32 61.7 us: along_z(): lax.ppermute(shard, 'expert', [(i, (i + 2 * by) % length) for i in range(...]
    ppermute x2 -> x38, starting transfers between devices: 3.29 us -> 64.8 us  [the longest x32 59.6 us: along_z(): lax.ppermute(shard, 'expert', [(i, (i + 2 * by) % length) for i in range(...]
    all_gather x2 -> x0, waiting for transfers between devices: 44.7 us -> none  [per_device(): lax.all_gather(normed, 'expert', axis=0, tiled=True)]
    dot_general x4 -> x0, matrix products: 40.8 us -> none  [the longest x2 28.5 us: expert_share(): product = jnp.dot(hidden, down_full, preferred_element_type=jnp.float32)]
    all_gather x2 -> x0, blocking collectives: 32.7 us -> none  [per_device(): lax.all_gather(weight_table, 'expert', axis=0, tiled=True)]
    pallas_call x0 -> x4, Pallas kernels: none -> 28.8 us  [the longest x2 28.6 us: experts_share(): pl.pallas_call(kernel, in_specs=[smem] * 3 + [vmem] * len(operands), out_...]
    mul x3 -> x0, local copies, waits for them, and re-layouts: 10.4 us -> none  [dequantize(): blocked * factor[:, None, :, None]]
  transfers between devices with their start and end apart: 6 -> 38, of which waited for: 6 -> 20; matrix products, arithmetic and copies ran while one was open for 1% -> 2% of each run, Pallas kernels for 0% -> 0%
where the time goes in v1:
time: 185 us; the launch traced here: 184 us
  waiting for transfers between devices  81.5 us (44%)
  starting transfers between devices  64.8 us (35%)
  Pallas kernels  28.8 us (16%)
  local copies, waits for them, and re-layouts  5.88 us (3%)
  other arithmetic  3.39 us (2%)
    ppermute x32, waiting for transfers between devices, along_z(): lax.ppermute(shard, 'expert', [(i, (i + 2 * by) % length) for i in range(...  61.7 us
    ppermute x32, starting transfers between devices, along_z(): lax.ppermute(shard, 'expert', [(i, (i + 2 * by) % length) for i in range(...  59.6 us
    pallas_call x2, Pallas kernels, experts_share(): pl.pallas_call(kernel, in_specs=[smem] * 3 + [vmem] * len(operands), out_...  28.6 us
    ppermute x2, waiting for transfers between devices, next_section(): lax.ppermute(shard, 'section', [(i, (i + 1) % length) for i in range(leng...  16.9 us
    unnamed x11, local copies, waits for them, and re-layouts  5.51 us
    ppermute x2, starting transfers between devices, next_section(): lax.ppermute(shard, 'section', [(i, (i + 1) % length) for i in range(leng...  4.34 us
  transfers between devices with their start and end apart: 38, of which 20 were waited for; matrix products, arithmetic and copies ran while one was open for 2% of the time, Pallas kernels for 0%

profile of v1, /device:TPU:0, one launch (start us, length us, event | category | flops | bytes accessed | tf_op | source)
XLA Modules:
  0.0 184.5 jit_solution(7908933524470511819)
XLA Ops:
  2.9 4.6 %collective-permute-start.4 = (bf16[16,7296]{1,0:T(8,128)(2,1)S(1)}, bf16[16,7296]{1,0:T(8,128)(2,1)S(1)}, u32[]{:S(2)}, u32[]{:S(2)}) collective-permute-start(bf16[16,7296]{1,0:T(8,128)(2,1)S(1)} %fusion.1.refs_3_), channel_id=1, source_target_pairs={{0,12},{1,13},{2,14},{3,15},{4,0},{5,1},{6,2},{7,3},{8,4},{9,5},{1... | collective-permute-start | bytes 700424 | tf_op jit(solution)/shard_map/ppermute | solution.py:18
  8.8 2.8 %collective-permute-done.refs_2_ = f32[336]{0:T(512)S(1)} collective-permute-done((f32[336]{0:T(512)S(1)}, f32[336]{0:T(512)S(1)}, u32[]{:S(2)}, u32[]{:S(2)}) %collective-permute-start) | collective-permute-done | bytes 1376 | tf_op jit(solution)/shard_map/ppermute | solution.py:25
  13.2 3.9 %collective-permute-done.4.refs_7_ = bf16[16,7296]{1,0:T(8,128)(2,1)S(1)} collective-permute-done((bf16[16,7296]{1,0:T(8,128)(2,1)S(1)}, bf16[16,7296]{1,0:T(8,128)(2,1)S(1)}, u32[]{:S(2)}, u32[]{:S(2)}) %collective-permute-start.4) | collective-permute-done | bytes 233504 | tf_op jit(solution)/shard_map/ppermute | solution.py:18
  17.1 4.9 %collective-permute-start.2 = (bf16[16,7296]{1,0:T(8,128)(2,1)S(1)}, bf16[16,7296]{1,0:T(8,128)(2,1)S(1)}, u32[]{:S(2)}, u32[]{:S(2)}) collective-permute-start(bf16[16,7296]{1,0:T(8,128)(2,1)S(1)} %fusion.1.refs_3_), channel_id=1, source_target_pairs={{0,14},{1,15},{2,0},{3,1},{4,2},{5,3},{6,4},{7,5},{8,6},{9,7},{10,... | collective-permute-start | bytes 700424 | tf_op jit(solution)/shard_map/ppermute | solution.py:18
  23.6 4.6 %collective-permute-start.1 = (bf16[16,7296]{1,0:T(8,128)(2,1)S(1)}, bf16[16,7296]{1,0:T(8,128)(2,1)S(1)}, u32[]{:S(2)}, u32[]{:S(2)}) collective-permute-start(bf16[16,7296]{1,0:T(8,128)(2,1)S(1)} %fusion.1.refs_3_), channel_id=1, source_target_pairs={{0,2},{1,3},{2,4},{3,5},{4,6},{5,7},{6,8},{7,9},{8,10},{9,11},{10,... | collective-permute-start | bytes 700424 | tf_op jit(solution)/shard_map/ppermute | solution.py:18
  28.3 2.9 %collective-permute-start.8 = (bf16[16,3712]{1,0:T(8,128)(2,1)S(1)}, bf16[16,3712]{1,0:T(8,128)(2,1)S(1)}, u32[]{:S(2)}, u32[]{:S(2)}) collective-permute-start(bf16[16,3712]{1,0:T(8,128)(2,1)S(1)} %slice.17), channel_id=1, source_target_pairs={{0,12},{1,13},{2,14},{3,15},{4,0},{5,1},{6,2},{7,3},{8,4},{9,5},{1... | collective-permute-start | bytes 356360 | tf_op jit(solution)/shard_map/ppermute | solution.py:18
  31.2 3.5 %collective-permute-done.1.refs_4_ = bf16[16,7296]{1,0:T(8,128)(2,1)S(1)} collective-permute-done((bf16[16,7296]{1,0:T(8,128)(2,1)S(1)}, bf16[16,7296]{1,0:T(8,128)(2,1)S(1)}, u32[]{:S(2)}, u32[]{:S(2)}) %collective-permute-start.1) | collective-permute-done | bytes 233504 | tf_op jit(solution)/shard_map/ppermute | solution.py:18
  35.2 8.0 %collective-permute-done.7.refs_10_ = bf16[16,3584]{1,0:T(8,128)(2,1)S(1)} collective-permute-done((bf16[16,3584]{1,0:T(8,128)(2,1)S(1)}, bf16[16,3584]{1,0:T(8,128)(2,1)S(1)}, u32[]{:S(2)}, u32[]{:S(2)}) %collective-permute-start.7) | collective-permute-done | bytes 114720 | tf_op jit(solution)/shard_map/ppermute | solution.py:18
  45.3 4.0 %collective-permute-done.6.refs_9_ = bf16[16,7296]{1,0:T(8,128)(2,1)S(1)} collective-permute-done((bf16[16,7296]{1,0:T(8,128)(2,1)S(1)}, bf16[16,7296]{1,0:T(8,128)(2,1)S(1)}, u32[]{:S(2)}, u32[]{:S(2)}) %collective-permute-start.6) | collective-permute-done | bytes 233504 | tf_op jit(solution)/shard_map/ppermute | solution.py:18
  53.3 14.1 %experts_share.2 = (bf16[16,7168]{1,0:T(8,128)(2,1)S(1)}, bf16[16,7168]{1,0:T(8,128)(2,1)S(1)}, bf16[16,7168]{1,0:T(8,128)(2,1)S(1)}, bf16[16,7168]{1,0:T(8,128)...) custom-call(s32[1]{0:T(128)} %bitcast.1.refs_0_, ...), custom_call_target="tpu_custom_call" | custom-call | flops 2818572288 | bytes 22020096 | tf_op jit(solution)/shard_map/experts_share/pallas_call | solution.py:224
  69.6 2.9 %collective-permute-start.17 = (bf16[16,3584]{1,0:T(8,128)(2,1)S(1)}, bf16[16,3584]{1,0:T(8,128)(2,1)S(1)}, u32[]{:S(2)}, u32[]{:S(2)}) collective-permute-start(bf16[16,3584]{1,0:T(8,128)(2,1)S(1)} %get-tuple-element.36), channel_id=1, source_target_pairs={{0,4},{1,5},{2,6},{3,7},{4,8},{5,9},{6,10},{7,11},{8,12},{9,13},{1... | collective-permute-start | bytes 344072 | tf_op jit(solution)/shard_map/ppermute | solution.py:18
  72.5 2.5 %collective-permute-start.12 = (bf16[16,7168]{1,0:T(8,128)(2,1)S(1)}, bf16[16,7168]{1,0:T(8,128)(2,1)S(1)}, u32[]{:S(2)}, u32[]{:S(2)}) collective-permute-start(bf16[16,7168]{1,0:T(8,128)(2,1)S(1)} %get-tuple-element.29), channel_id=1, source_target_pairs={{0,14},{1,15},{2,0},{3,1},{4,2},{5,3},{6,4},{7,5},{8,6},{9,7},{10,... | collective-permute-start | bytes 688136 | tf_op jit(solution)/shard_map/ppermute | solution.py:18
  77.0 3.7 %collective-permute-start.13 = (bf16[16,7168]{1,0:T(8,128)(2,1)S(1)}, bf16[16,7168]{1,0:T(8,128)(2,1)S(1)}, u32[]{:S(2)}, u32[]{:S(2)}) collective-permute-start(bf16[16,7168]{1,0:T(8,128)(2,1)S(1)} %get-tuple-element.30), channel_id=1, source_target_pairs={{0,2},{1,3},{2,4},{3,5},{4,6},{5,7},{6,8},{7,9},{8,10},{9,11},{10,... | collective-permute-start | bytes 688136 | tf_op jit(solution)/shard_map/ppermute | solution.py:18
  80.9 3.1 %collective-permute-start.18 = (bf16[16,7168]{1,0:T(8,128)(2,1)S(1)}, bf16[16,7168]{1,0:T(8,128)(2,1)S(1)}, u32[]{:S(2)}, u32[]{:S(2)}) collective-permute-start(bf16[16,7168]{1,0:T(8,128)(2,1)S(1)} %get-tuple-element.37), channel_id=1, source_target_pairs={{0,12},{1,13},{2,14},{3,15},{4,0},{5,1},{6,2},{7,3},{8,4},{9,5},{1... | collective-permute-start | bytes 688136 | tf_op jit(solution)/shard_map/ppermute | solution.py:18
  85.3 2.4 %collective-permute-done.13 = bf16[16,7168]{1,0:T(8,128)(2,1)S(1)} collective-permute-done((bf16[16,7168]{1,0:T(8,128)(2,1)S(1)}, bf16[16,7168]{1,0:T(8,128)(2,1)S(1)}, u32[]{:S(2)}, u32[]{:S(2)}) %collective-permute-start.13) | collective-permute-done | bytes 229408 | tf_op jit(solution)/shard_map/ppermute | solution.py:18
  87.7 2.7 %collective-permute-done.18 = bf16[16,7168]{1,0:T(8,128)(2,1)S(1)} collective-permute-done((bf16[16,7168]{1,0:T(8,128)(2,1)S(1)}, bf16[16,7168]{1,0:T(8,128)(2,1)S(1)}, u32[]{:S(2)}, u32[]{:S(2)}) %collective-permute-start.18) | collective-permute-done | bytes 229408 | tf_op jit(solution)/shard_map/ppermute | solution.py:18
  90.5 3.5 %collective-permute-done.19 = bf16[16,7168]{1,0:T(8,128)(2,1)S(1)} collective-permute-done((bf16[16,7168]{1,0:T(8,128)(2,1)S(1)}, bf16[16,7168]{1,0:T(8,128)(2,1)S(1)}, u32[]{:S(2)}, u32[]{:S(2)}) %collective-permute-start.19) | collective-permute-done | bytes 229408 | tf_op jit(solution)/shard_map/ppermute | solution.py:18
  94.1 4.3 %collective-permute-start.20 = (bf16[16,7168]{1,0:T(8,128)(2,1)S(1)}, bf16[16,7168]{1,0:T(8,128)(2,1)S(1)}, u32[]{:S(2)}, u32[]{:S(2)}) collective-permute-start(bf16[16,7168]{1,0:T(8,128)(2,1)S(1)} %add_convert_fusion.1), channel_id=1, source_target_pairs={{0,16},{16,32},{32,48},{48,64},{64,80},{80,96},{96,112},{112,128},... | collective-permute-start | bytes 688136 | tf_op jit(solution)/shard_map/ppermute | solution.py:30
  98.4 7.6 %collective-permute-done.20.refs_3_ = bf16[16,7168]{1,0:T(8,128)(2,1)S(1)} collective-permute-done((bf16[16,7168]{1,0:T(8,128)(2,1)S(1)}, bf16[16,7168]{1,0:T(8,128)(2,1)S(1)}, u32[]{:S(2)}, u32[]{:S(2)}) %collective-permute-start.20) | collective-permute-done | bytes 229408 | tf_op jit(solution)/shard_map/ppermute | solution.py:30
  106.0 2.9 %collective-permute-start.23 = (bf16[16,7168]{1,0:T(8,128)(2,1)S(1)}, bf16[16,7168]{1,0:T(8,128)(2,1)S(1)}, u32[]{:S(2)}, u32[]{:S(2)}) collective-permute-start(bf16[16,7168]{1,0:T(8,128)(2,1)S(1)} %collective-permute-done.20.refs_3_), channel_id=1, source_target_pairs={{0,4},{1,5},{2,6},{3,7},{4,8},{5,9},{6,10},{7,11},{8,12},{9,13},{1... | collective-permute-start | bytes 688136 | tf_op jit(solution)/shard_map/ppermute | solution.py:18
  111.0 5.0 %collective-permute-done.24.refs_7_ = bf16[16,7168]{1,0:T(8,128)(2,1)S(1)} collective-permute-done((bf16[16,7168]{1,0:T(8,128)(2,1)S(1)}, bf16[16,7168]{1,0:T(8,128)(2,1)S(1)}, u32[]{:S(2)}, u32[]{:S(2)}) %collective-permute-start.24) | collective-permute-done | bytes 229408 | tf_op jit(solution)/shard_map/ppermute | solution.py:18
  116.0 4.1 %collective-permute-start.26 = (bf16[16,7168]{1,0:T(8,128)(2,1)S(1)}, bf16[16,7168]{1,0:T(8,128)(2,1)S(1)}, u32[]{:S(2)}, u32[]{:S(2)}) collective-permute-start(bf16[16,7168]{1,0:T(8,128)(2,1)S(1)} %collective-permute-done.24.refs_7_), channel_id=1, source_target_pairs={{0,14},{1,15},{2,0},{3,1},{4,2},{5,3},{6,4},{7,5},{8,6},{9,7},{10,... | collective-permute-start | bytes 688136 | tf_op jit(solution)/shard_map/ppermute | solution.py:18
  124.0 2.9 %collective-permute-done.28.refs_11_ = bf16[16,3584]{1,0:T(8,128)(2,1)S(1)} collective-permute-done((bf16[16,3584]{1,0:T(8,128)(2,1)S(1)}, bf16[16,3584]{1,0:T(8,128)(2,1)S(1)}, u32[]{:S(2)}, u32[]{:S(2)}) %collective-permute-start.28) | collective-permute-done | bytes 114720 | tf_op jit(solution)/shard_map/ppermute | solution.py:18
  127.0 3.0 %collective-permute-done.27.refs_10_ = bf16[16,3584]{1,0:T(8,128)(2,1)S(1)} collective-permute-done((bf16[16,3584]{1,0:T(8,128)(2,1)S(1)}, bf16[16,3584]{1,0:T(8,128)(2,1)S(1)}, u32[]{:S(2)}, u32[]{:S(2)}) %collective-permute-start.27) | collective-permute-done | bytes 114720 | tf_op jit(solution)/shard_map/ppermute | solution.py:18
  132.1 14.4 %experts_share.3 = (bf16[16,7168]{1,0:T(8,128)(2,1)S(1)}, bf16[16,7168]{1,0:T(8,128)(2,1)S(1)}, bf16[16,7168]{1,0:T(8,128)(2,1)S(1)}, bf16[16,7168]{1,0:T(8,128)...) custom-call(s32[1]{0:T(128)} %bitcast.9.refs_0_, ...), custom_call_target="tpu_custom_call" | custom-call | flops 2818572288 | bytes 22020096 | tf_op jit(solution)/shard_map/experts_share/pallas_call | solution.py:224
  149.3 2.7 %collective-permute-start.34 = (bf16[16,3584]{1,0:T(8,128)(2,1)S(1)}, bf16[16,3584]{1,0:T(8,128)(2,1)S(1)}, u32[]{:S(2)}, u32[]{:S(2)}) collective-permute-start(bf16[16,3584]{1,0:T(8,128)(2,1)S(1)} %get-tuple-element.48), channel_id=1, source_target_pairs={{0,4},{1,5},{2,6},{3,7},{4,8},{5,9},{6,10},{7,11},{8,12},{9,13},{1... | collective-permute-start | bytes 344072 | tf_op jit(solution)/shard_map/ppermute | solution.py:18
  152.0 2.7 %collective-permute-start.29 = (bf16[16,7168]{1,0:T(8,128)(2,1)S(1)}, bf16[16,7168]{1,0:T(8,128)(2,1)S(1)}, u32[]{:S(2)}, u32[]{:S(2)}) collective-permute-start(bf16[16,7168]{1,0:T(8,128)(2,1)S(1)} %get-tuple-element.41), channel_id=1, source_target_pairs={{0,14},{1,15},{2,0},{3,1},{4,2},{5,3},{6,4},{7,5},{8,6},{9,7},{10,... | collective-permute-start | bytes 688136 | tf_op jit(solution)/shard_map/ppermute | solution.py:18
  154.7 6.4 %collective-permute-done.33.left = bf16[16,3584]{1,0:T(8,128)(2,1)S(1)} collective-permute-done((bf16[16,3584]{1,0:T(8,128)(2,1)S(1)}, bf16[16,3584]{1,0:T(8,128)(2,1)S(1)}, u32[]{:S(2)}, u32[]{:S(2)}) %collective-permute-start.33) | collective-permute-done | bytes 114720 | tf_op jit(solution)/shard_map/ppermute | solution.py:18
  161.3 2.3 %collective-permute-start.35 = (bf16[16,7168]{1,0:T(8,128)(2,1)S(1)}, bf16[16,7168]{1,0:T(8,128)(2,1)S(1)}, u32[]{:S(2)}, u32[]{:S(2)}) collective-permute-start(bf16[16,7168]{1,0:T(8,128)(2,1)S(1)} %get-tuple-element.49), channel_id=1, source_target_pairs={{0,12},{1,13},{2,14},{3,15},{4,0},{5,1},{6,2},{7,3},{8,4},{9,5},{1... | collective-permute-start | bytes 688136 | tf_op jit(solution)/shard_map/ppermute | solution.py:18
  164.3 4.1 %collective-permute-done.30 = bf16[16,7168]{1,0:T(8,128)(2,1)S(1)} collective-permute-done((bf16[16,7168]{1,0:T(8,128)(2,1)S(1)}, bf16[16,7168]{1,0:T(8,128)(2,1)S(1)}, u32[]{:S(2)}, u32[]{:S(2)}) %collective-permute-start.30) | collective-permute-done | bytes 229408 | tf_op jit(solution)/shard_map/ppermute | solution.py:18
  168.3 5.9 %collective-permute-done.36 = bf16[16,7168]{1,0:T(8,128)(2,1)S(1)} collective-permute-done((bf16[16,7168]{1,0:T(8,128)(2,1)S(1)}, bf16[16,7168]{1,0:T(8,128)(2,1)S(1)}, u32[]{:S(2)}, u32[]{:S(2)}) %collective-permute-start.36) | collective-permute-done | bytes 229408 | tf_op jit(solution)/shard_map/ppermute | solution.py:18
  174.5 9.3 %collective-permute-done.37 = bf16[16,7168]{1,0:T(8,128)(2,1)S(1)} collective-permute-done((bf16[16,7168]{1,0:T(8,128)(2,1)S(1)}, bf16[16,7168]{1,0:T(8,128)(2,1)S(1)}, u32[]{:S(2)}, u32[]{:S(2)}) %collective-permute-start.37) | collective-permute-done | bytes 229408 | tf_op jit(solution)/shard_map/ppermute | solution.py:30
  (72 shorter events, 32.4 us)
Async XLA Ops:
  0.0 50.5 %collective-permute-start.9 = (bf16[7168,256]{1,0:T(8,128)(2,1)}, bf16[7168,256]{1,0:T(8,128)(2,1)}, u32[]{:S(2)}, u32[]{:S(2)}) collective-permute-start(bf16[7168,256]{1,0:T(8,128)(2,1)} %bitcast.17), channel_id=1, source_target_pairs={{0,1},{1,0},{2,3},{3,2},{4,5},{5,4},{6,7},{7,6},{8,9},{9,8},{10,11... | collective-permute-start | bytes 11010056 | tf_op jit(solution)/shard_map/ppermute | solution.py:25
  0.0 50.5 %collective-permute-start.10 = (bf16[7168,256]{1,0:T(8,128)(2,1)}, bf16[7168,256]{1,0:T(8,128)(2,1)}, u32[]{:S(2)}, u32[]{:S(2)}) collective-permute-start(bf16[7168,256]{1,0:T(8,128)(2,1)} %bitcast.20), channel_id=1, source_target_pairs={{0,1},{1,0},{2,3},{3,2},{4,5},{5,4},{6,7},{7,6},{8,9},{9,8},{10,11... | collective-permute-start | bytes 11010056 | tf_op jit(solution)/shard_map/ppermute | solution.py:25
  0.5 50.0 %collective-permute-start.11 = (bf16[256,7168]{1,0:T(8,128)(2,1)}, bf16[256,7168]{1,0:T(8,128)(2,1)}, u32[]{:S(2)}, u32[]{:S(2)}) collective-permute-start(bf16[256,7168]{1,0:T(8,128)(2,1)} %bitcast.23), channel_id=1, source_target_pairs={{0,1},{1,0},{2,3},{3,2},{4,5},{5,4},{6,7},{7,6},{8,9},{9,8},{10,11... | collective-permute-start | bytes 11010056 | tf_op jit(solution)/shard_map/ppermute | solution.py:25
  2.9 14.2 %collective-permute-start.4 = (bf16[16,7296]{1,0:T(8,128)(2,1)S(1)}, bf16[16,7296]{1,0:T(8,128)(2,1)S(1)}, u32[]{:S(2)}, u32[]{:S(2)}) collective-permute-start(bf16[16,7296]{1,0:T(8,128)(2,1)S(1)} %fusion.1.refs_3_), channel_id=1, source_target_pairs={{0,12},{1,13},{2,14},{3,15},{4,0},{5,1},{6,2},{7,3},{8,4},{9,5},{1... | collective-permute-start | bytes 700424 | tf_op jit(solution)/shard_map/ppermute | solution.py:18
  11.7 12.0 %collective-permute-start.3 = (bf16[16,7296]{1,0:T(8,128)(2,1)S(1)}, bf16[16,7296]{1,0:T(8,128)(2,1)S(1)}, u32[]{:S(2)}, u32[]{:S(2)}) collective-permute-start(bf16[16,7296]{1,0:T(8,128)(2,1)S(1)} %fusion.1.refs_3_), channel_id=1, source_target_pairs={{0,4},{1,5},{2,6},{3,7},{4,8},{5,9},{6,10},{7,11},{8,12},{9,13},{1... | collective-permute-start | bytes 700424 | tf_op jit(solution)/shard_map/ppermute | solution.py:18
  17.1 11.1 %collective-permute-start.2 = (bf16[16,7296]{1,0:T(8,128)(2,1)S(1)}, bf16[16,7296]{1,0:T(8,128)(2,1)S(1)}, u32[]{:S(2)}, u32[]{:S(2)}) collective-permute-start(bf16[16,7296]{1,0:T(8,128)(2,1)S(1)} %fusion.1.refs_3_), channel_id=1, source_target_pairs={{0,14},{1,15},{2,0},{3,1},{4,2},{5,3},{6,4},{7,5},{8,6},{9,7},{10,... | collective-permute-start | bytes 700424 | tf_op jit(solution)/shard_map/ppermute | solution.py:18
  23.6 11.0 %collective-permute-start.1 = (bf16[16,7296]{1,0:T(8,128)(2,1)S(1)}, bf16[16,7296]{1,0:T(8,128)(2,1)S(1)}, u32[]{:S(2)}, u32[]{:S(2)}) collective-permute-start(bf16[16,7296]{1,0:T(8,128)(2,1)S(1)} %fusion.1.refs_3_), channel_id=1, source_target_pairs={{0,2},{1,3},{2,4},{3,5},{4,6},{5,7},{6,8},{7,9},{8,10},{9,11},{10,... | collective-permute-start | bytes 700424 | tf_op jit(solution)/shard_map/ppermute | solution.py:18
  28.3 15.0 %collective-permute-start.8 = (bf16[16,3712]{1,0:T(8,128)(2,1)S(1)}, bf16[16,3712]{1,0:T(8,128)(2,1)S(1)}, u32[]{:S(2)}, u32[]{:S(2)}) collective-permute-start(bf16[16,3712]{1,0:T(8,128)(2,1)S(1)} %slice.17), channel_id=1, source_target_pairs={{0,12},{1,13},{2,14},{3,15},{4,0},{5,1},{6,2},{7,3},{8,4},{9,5},{1... | collective-permute-start | bytes 356360 | tf_op jit(solution)/shard_map/ppermute | solution.py:18
  34.6 8.6 %collective-permute-start.7 = (bf16[16,3584]{1,0:T(8,128)(2,1)S(1)}, bf16[16,3584]{1,0:T(8,128)(2,1)S(1)}, u32[]{:S(2)}, u32[]{:S(2)}) collective-permute-start(bf16[16,3584]{1,0:T(8,128)(2,1)S(1)} %slice.16), channel_id=1, source_target_pairs={{0,4},{1,5},{2,6},{3,7},{4,8},{5,9},{6,10},{7,11},{8,12},{9,13},{1... | collective-permute-start | bytes 344072 | tf_op jit(solution)/shard_map/ppermute | solution.py:18
  67.5 13.2 %collective-permute-start.14 = (bf16[16,7168]{1,0:T(8,128)(2,1)S(1)}, bf16[16,7168]{1,0:T(8,128)(2,1)S(1)}, u32[]{:S(2)}, u32[]{:S(2)}) collective-permute-start(bf16[16,7168]{1,0:T(8,128)(2,1)S(1)} %get-tuple-element.33), channel_id=1, source_target_pairs={{0,14},{1,15},{2,0},{3,1},{4,2},{5,3},{6,4},{7,5},{8,6},{9,7},{10,... | collective-permute-start | bytes 688136 | tf_op jit(solution)/shard_map/ppermute | solution.py:18
  67.6 13.1 %collective-permute-start.15 = (bf16[16,7168]{1,0:T(8,128)(2,1)S(1)}, bf16[16,7168]{1,0:T(8,128)(2,1)S(1)}, u32[]{:S(2)}, u32[]{:S(2)}) collective-permute-start(bf16[16,7168]{1,0:T(8,128)(2,1)S(1)} %get-tuple-element.34), channel_id=1, source_target_pairs={{0,2},{1,3},{2,4},{3,5},{4,6},{5,7},{6,8},{7,9},{8,10},{9,11},{10,... | collective-permute-start | bytes 688136 | tf_op jit(solution)/shard_map/ppermute | solution.py:18
  69.6 7.5 %collective-permute-start.16 = (bf16[16,3584]{1,0:T(8,128)(2,1)S(1)}, bf16[16,3584]{1,0:T(8,128)(2,1)S(1)}, u32[]{:S(2)}, u32[]{:S(2)}) collective-permute-start(bf16[16,3584]{1,0:T(8,128)(2,1)S(1)} %get-tuple-element.35), channel_id=1, source_target_pairs={{0,12},{1,13},{2,14},{3,15},{4,0},{5,1},{6,2},{7,3},{8,4},{9,5},{1... | collective-permute-start | bytes 344072 | tf_op jit(solution)/shard_map/ppermute | solution.py:18
  69.6 11.1 %collective-permute-start.17 = (bf16[16,3584]{1,0:T(8,128)(2,1)S(1)}, bf16[16,3584]{1,0:T(8,128)(2,1)S(1)}, u32[]{:S(2)}, u32[]{:S(2)}) collective-permute-start(bf16[16,3584]{1,0:T(8,128)(2,1)S(1)} %get-tuple-element.36), channel_id=1, source_target_pairs={{0,4},{1,5},{2,6},{3,7},{4,8},{5,9},{6,10},{7,11},{8,12},{9,13},{1... | collective-permute-start | bytes 344072 | tf_op jit(solution)/shard_map/ppermute | solution.py:18
  72.5 12.8 %collective-permute-start.12 = (bf16[16,7168]{1,0:T(8,128)(2,1)S(1)}, bf16[16,7168]{1,0:T(8,128)(2,1)S(1)}, u32[]{:S(2)}, u32[]{:S(2)}) collective-permute-start(bf16[16,7168]{1,0:T(8,128)(2,1)S(1)} %get-tuple-element.29), channel_id=1, source_target_pairs={{0,14},{1,15},{2,0},{3,1},{4,2},{5,3},{6,4},{7,5},{8,6},{9,7},{10,... | collective-permute-start | bytes 688136 | tf_op jit(solution)/shard_map/ppermute | solution.py:18
  77.0 10.7 %collective-permute-start.13 = (bf16[16,7168]{1,0:T(8,128)(2,1)S(1)}, bf16[16,7168]{1,0:T(8,128)(2,1)S(1)}, u32[]{:S(2)}, u32[]{:S(2)}) collective-permute-start(bf16[16,7168]{1,0:T(8,128)(2,1)S(1)} %get-tuple-element.30), channel_id=1, source_target_pairs={{0,2},{1,3},{2,4},{3,5},{4,6},{5,7},{6,8},{7,9},{8,10},{9,11},{10,... | collective-permute-start | bytes 688136 | tf_op jit(solution)/shard_map/ppermute | solution.py:18
  80.9 9.6 %collective-permute-start.18 = (bf16[16,7168]{1,0:T(8,128)(2,1)S(1)}, bf16[16,7168]{1,0:T(8,128)(2,1)S(1)}, u32[]{:S(2)}, u32[]{:S(2)}) collective-permute-start(bf16[16,7168]{1,0:T(8,128)(2,1)S(1)} %get-tuple-element.37), channel_id=1, source_target_pairs={{0,12},{1,13},{2,14},{3,15},{4,0},{5,1},{6,2},{7,3},{8,4},{9,5},{1... | collective-permute-start | bytes 688136 | tf_op jit(solution)/shard_map/ppermute | solution.py:18
  83.9 10.0 %collective-permute-start.19 = (bf16[16,7168]{1,0:T(8,128)(2,1)S(1)}, bf16[16,7168]{1,0:T(8,128)(2,1)S(1)}, u32[]{:S(2)}, u32[]{:S(2)}) collective-permute-start(bf16[16,7168]{1,0:T(8,128)(2,1)S(1)} %get-tuple-element.38), channel_id=1, source_target_pairs={{0,4},{1,5},{2,6},{3,7},{4,8},{5,9},{6,10},{7,11},{8,12},{9,13},{1... | collective-permute-start | bytes 688136 | tf_op jit(solution)/shard_map/ppermute | solution.py:18
  94.1 11.9 %collective-permute-start.20 = (bf16[16,7168]{1,0:T(8,128)(2,1)S(1)}, bf16[16,7168]{1,0:T(8,128)(2,1)S(1)}, u32[]{:S(2)}, u32[]{:S(2)}) collective-permute-start(bf16[16,7168]{1,0:T(8,128)(2,1)S(1)} %add_convert_fusion.1), channel_id=1, source_target_pairs={{0,16},{16,32},{32,48},{48,64},{64,80},{80,96},{96,112},{112,128},... | collective-permute-start | bytes 688136 | tf_op jit(solution)/shard_map/ppermute | solution.py:30
  106.0 10.0 %collective-permute-start.24 = (bf16[16,7168]{1,0:T(8,128)(2,1)S(1)}, bf16[16,7168]{1,0:T(8,128)(2,1)S(1)}, u32[]{:S(2)}, u32[]{:S(2)}) collective-permute-start(bf16[16,7168]{1,0:T(8,128)(2,1)S(1)} %collective-permute-done.20.refs_3_), channel_id=1, source_target_pairs={{0,12},{1,13},{2,14},{3,15},{4,0},{5,1},{6,2},{7,3},{8,4},{9,5},{1... | collective-permute-start | bytes 688136 | tf_op jit(solution)/shard_map/ppermute | solution.py:18
  106.0 14.1 %collective-permute-start.23 = (bf16[16,7168]{1,0:T(8,128)(2,1)S(1)}, bf16[16,7168]{1,0:T(8,128)(2,1)S(1)}, u32[]{:S(2)}, u32[]{:S(2)}) collective-permute-start(bf16[16,7168]{1,0:T(8,128)(2,1)S(1)} %collective-permute-done.20.refs_3_), channel_id=1, source_target_pairs={{0,4},{1,5},{2,6},{3,7},{4,8},{5,9},{6,10},{7,11},{8,12},{9,13},{1... | collective-permute-start | bytes 688136 | tf_op jit(solution)/shard_map/ppermute | solution.py:18
  108.9 12.8 %collective-permute-start.22 = (bf16[16,7168]{1,0:T(8,128)(2,1)S(1)}, bf16[16,7168]{1,0:T(8,128)(2,1)S(1)}, u32[]{:S(2)}, u32[]{:S(2)}) collective-permute-start(bf16[16,7168]{1,0:T(8,128)(2,1)S(1)} %collective-permute-done.20.refs_3_), channel_id=1, source_target_pairs={{0,14},{1,15},{2,0},{3,1},{4,2},{5,3},{6,4},{7,5},{8,6},{9,7},{10,... | collective-permute-start | bytes 688136 | tf_op jit(solution)/shard_map/ppermute | solution.py:18
  109.9 14.1 %collective-permute-start.21 = (bf16[16,7168]{1,0:T(8,128)(2,1)S(1)}, bf16[16,7168]{1,0:T(8,128)(2,1)S(1)}, u32[]{:S(2)}, u32[]{:S(2)}) collective-permute-start(bf16[16,7168]{1,0:T(8,128)(2,1)S(1)} %collective-permute-done.20.refs_3_), channel_id=1, source_target_pairs={{0,2},{1,3},{2,4},{3,5},{4,6},{5,7},{6,8},{7,9},{8,10},{9,11},{10,... | collective-permute-start | bytes 688136 | tf_op jit(solution)/shard_map/ppermute | solution.py:18
  116.0 14.0 %collective-permute-start.26 = (bf16[16,7168]{1,0:T(8,128)(2,1)S(1)}, bf16[16,7168]{1,0:T(8,128)(2,1)S(1)}, u32[]{:S(2)}, u32[]{:S(2)}) collective-permute-start(bf16[16,7168]{1,0:T(8,128)(2,1)S(1)} %collective-permute-done.24.refs_7_), channel_id=1, source_target_pairs={{0,14},{1,15},{2,0},{3,1},{4,2},{5,3},{6,4},{7,5},{8,6},{9,7},{10,... | collective-permute-start | bytes 688136 | tf_op jit(solution)/shard_map/ppermute | solution.py:18
  120.1 9.9 %collective-permute-start.25 = (bf16[16,7168]{1,0:T(8,128)(2,1)S(1)}, bf16[16,7168]{1,0:T(8,128)(2,1)S(1)}, u32[]{:S(2)}, u32[]{:S(2)}) collective-permute-start(bf16[16,7168]{1,0:T(8,128)(2,1)S(1)} %collective-permute-done.23.refs_6_), channel_id=1, source_target_pairs={{0,2},{1,3},{2,4},{3,5},{4,6},{5,7},{6,8},{7,9},{8,10},{9,11},{10,... | collective-permute-start | bytes 688136 | tf_op jit(solution)/shard_map/ppermute | solution.py:18
  121.7 8.3 %collective-permute-start.27 = (bf16[16,3584]{1,0:T(8,128)(2,1)S(1)}, bf16[16,3584]{1,0:T(8,128)(2,1)S(1)}, u32[]{:S(2)}, u32[]{:S(2)}) collective-permute-start(bf16[16,3584]{1,0:T(8,128)(2,1)S(1)} %slice.18), channel_id=1, source_target_pairs={{0,4},{1,5},{2,6},{3,7},{4,8},{5,9},{6,10},{7,11},{8,12},{9,13},{1... | collective-permute-start | bytes 344072 | tf_op jit(solution)/shard_map/ppermute | solution.py:18
  146.5 14.6 %collective-permute-start.31 = (bf16[16,7168]{1,0:T(8,128)(2,1)S(1)}, bf16[16,7168]{1,0:T(8,128)(2,1)S(1)}, u32[]{:S(2)}, u32[]{:S(2)}) collective-permute-start(bf16[16,7168]{1,0:T(8,128)(2,1)S(1)} %get-tuple-element.45), channel_id=1, source_target_pairs={{0,14},{1,15},{2,0},{3,1},{4,2},{5,3},{6,4},{7,5},{8,6},{9,7},{10,... | collective-permute-start | bytes 688136 | tf_op jit(solution)/shard_map/ppermute | solution.py:18
  147.3 13.8 %collective-permute-start.32 = (bf16[16,7168]{1,0:T(8,128)(2,1)S(1)}, bf16[16,7168]{1,0:T(8,128)(2,1)S(1)}, u32[]{:S(2)}, u32[]{:S(2)}) collective-permute-start(bf16[16,7168]{1,0:T(8,128)(2,1)S(1)} %get-tuple-element.46), channel_id=1, source_target_pairs={{0,2},{1,3},{2,4},{3,5},{4,6},{5,7},{6,8},{7,9},{8,10},{9,11},{10,... | collective-permute-start | bytes 688136 | tf_op jit(solution)/shard_map/ppermute | solution.py:18
  149.1 12.0 %collective-permute-start.33 = (bf16[16,3584]{1,0:T(8,128)(2,1)S(1)}, bf16[16,3584]{1,0:T(8,128)(2,1)S(1)}, u32[]{:S(2)}, u32[]{:S(2)}) collective-permute-start(bf16[16,3584]{1,0:T(8,128)(2,1)S(1)} %get-tuple-element.47), channel_id=1, source_target_pairs={{0,12},{1,13},{2,14},{3,15},{4,0},{5,1},{6,2},{7,3},{8,4},{9,5},{1... | collective-permute-start | bytes 344072 | tf_op jit(solution)/shard_map/ppermute | solution.py:18
  149.3 11.8 %collective-permute-start.34 = (bf16[16,3584]{1,0:T(8,128)(2,1)S(1)}, bf16[16,3584]{1,0:T(8,128)(2,1)S(1)}, u32[]{:S(2)}, u32[]{:S(2)}) collective-permute-start(bf16[16,3584]{1,0:T(8,128)(2,1)S(1)} %get-tuple-element.48), channel_id=1, source_target_pairs={{0,4},{1,5},{2,6},{3,7},{4,8},{5,9},{6,10},{7,11},{8,12},{9,13},{1... | collective-permute-start | bytes 344072 | tf_op jit(solution)/shard_map/ppermute | solution.py:18
  152.0 12.3 %collective-permute-start.29 = (bf16[16,7168]{1,0:T(8,128)(2,1)S(1)}, bf16[16,7168]{1,0:T(8,128)(2,1)S(1)}, u32[]{:S(2)}, u32[]{:S(2)}) collective-permute-start(bf16[16,7168]{1,0:T(8,128)(2,1)S(1)} %get-tuple-element.41), channel_id=1, source_target_pairs={{0,14},{1,15},{2,0},{3,1},{4,2},{5,3},{6,4},{7,5},{8,6},{9,7},{10,... | collective-permute-start | bytes 688136 | tf_op jit(solution)/shard_map/ppermute | solution.py:18
  163.6 10.6 %collective-permute-start.36 = (bf16[16,7168]{1,0:T(8,128)(2,1)S(1)}, bf16[16,7168]{1,0:T(8,128)(2,1)S(1)}, u32[]{:S(2)}, u32[]{:S(2)}) collective-permute-start(bf16[16,7168]{1,0:T(8,128)(2,1)S(1)} %get-tuple-element.50), channel_id=1, source_target_pairs={{0,4},{1,5},{2,6},{3,7},{4,8},{5,9},{6,10},{7,11},{8,12},{9,13},{1... | collective-permute-start | bytes 688136 | tf_op jit(solution)/shard_map/ppermute | solution.py:18
  174.4 9.4 %collective-permute-start.37 = (bf16[16,7168]{1,0:T(8,128)(2,1)S(1)}, bf16[16,7168]{1,0:T(8,128)(2,1)S(1)}, u32[]{:S(2)}, u32[]{:S(2)}) collective-permute-start(bf16[16,7168]{1,0:T(8,128)(2,1)S(1)} %add_convert_fusion), channel_id=1, source_target_pairs={{0,16},{16,32},{32,48},{48,64},{64,80},{80,96},{96,112},{112,128},... | collective-permute-start | bytes 688136 | tf_op jit(solution)/shard_map/ppermute | solution.py:30
  (11 other events, 159.0 us)
